TPU v7x, 32 devices: a whole 2x2x4 slice. The times are simulated.
32 devices in a mesh: tile: 8 (over y, x, core), frame: 4 (over z).
Axes of the slice: x: 2, y: 2, z: 4, core: 2. Of those that a mesh axis runs over, the one named last changes fastest.
Arguments:
- frames: bfloat16 [8, 256, 512], P('frame', 'tile'), may hold values from -6 to 6
- row_shifts: int32 [512, 8], P('frame'), may hold values from -16 to 16, as said below
- column_shifts: int32 [512, 8], P('frame'), may hold values from -16 to 16, as said below
- frame_inverse_weight: float32 [8], replicated, may hold values from 0.05 to 0.5
- psf_rows: float32 [13], replicated, may hold values from 0.1 to 0.4
- psf_cols: float32 [13], replicated, may hold values from 0.1 to 0.4
Outputs:
- filtered: bfloat16 [512, 256, 512], P('frame', 'tile')
Inputs may be any that keep to these rules, and one draw needn't show every extreme that they name: row_shifts[v, f] = floor(r_v * (2 f - 7) / 7) for an integer row rate r_v per velocity; both extremes are reached. column_shifts follows the same law with an integer column rate c_v per velocity; both extremes are reached; the rate pairs (r_v, c_v) are distinct across all 512 velocities.
All inputs are finite; a program needn't handle non-finite values.
Results may differ from a plain program's by a relative error of at most 0.005.
Values may be sent and summed in bfloat16 or wider, within the bound.
No kernel may reach another device: no remote copies, remote signals or barrier semaphores. Data moves between devices by JAX's collectives and lax.ppermute only.
A program may use at most 64 MiB of HBM per device.

v0:
```python
import jax
import jax.numpy as jnp
from jax import lax
from jax.sharding import PartitionSpec as P

HALO = 16
RADIUS = 6


def extended_2(cells, sides, width):
    for axis, dim in sides:
        count = lax.axis_size(axis)
        ends = count - 1
        head = lax.slice_in_dim(cells, 0, width, axis=dim)
        tail = lax.slice_in_dim(cells, cells.shape[dim] - width, cells.shape[dim], axis=dim)
        cells = jnp.concatenate(
            [
                lax.ppermute(tail, axis, [(i, (i + 1) % count) for i in range(ends)]),
                cells,
                lax.ppermute(head, axis, [((i + 1) % count, i) for i in range(ends)]),
            ],
            axis=dim,
        )
    return cells


def shards(frames, row_shifts, column_shifts, frame_inverse_weight, psf_rows, psf_cols):
    rows = frames.shape[1]
    width = frames.shape[2]
    vel_count = row_shifts.shape[0]
    haloed = extended_2(frames, (("tile", 1),), HALO)
    stack_rows = haloed.shape[1] - 2 * HALO
    empty = jnp.zeros((vel_count, stack_rows, width), jnp.float32)
    piece = lax.all_gather(haloed, "frame", axis=0, tiled=True)

    def one_frame(index, acc):
        frame_image = jnp.pad(piece[index], ((0, 0), (HALO, HALO)))
        weight = lax.dynamic_index_in_dim(frame_inverse_weight, index, 0, keepdims=False)
        row_moves = lax.dynamic_index_in_dim(row_shifts, index, 1, keepdims=False)
        col_moves = lax.dynamic_index_in_dim(column_shifts, index, 1, keepdims=False)

        def window(row_move, col_move):
            return lax.dynamic_slice(
                frame_image, (HALO + row_move, HALO + col_move), (stack_rows, width)
            )

        moved = jax.vmap(window)(row_moves, col_moves)
        return acc + weight * moved.astype(jnp.float32)

    summed = lax.fori_loop(0, piece.shape[0], one_frame, empty)
    stacked = summed.astype(jnp.bfloat16)
    extended = extended_2(stacked, (("tile", 1),), RADIUS)
    rowpass = jnp.zeros((vel_count, rows, width), jnp.float32)
    for k in range(2 * RADIUS + 1):
        rowpass = rowpass + psf_rows[k] * extended[:, k : k + rows, :].astype(jnp.float32)
    wide_rows = jnp.pad(rowpass, ((0, 0), (0, 0), (RADIUS, RADIUS)))
    result = jnp.zeros((vel_count, rows, width), jnp.float32)
    for k in range(2 * RADIUS + 1):
        result = result + psf_cols[k] * wide_rows[:, :, k : k + width]
    return result.astype(jnp.bfloat16)


def solution(mesh):
    return jax.shard_map(
        shards,
        mesh=mesh,
        in_specs=(P("frame", "tile", None), P("frame", None), P("frame", None), P(), P(), P()),
        out_specs=P("frame", "tile", None),
        check_vma=False,
    )
```

profile of v0, /device:TPU:0, one launch (start us, length us, event | category | flops | bytes accessed | tf_op | source)
XLA Modules:
  0.0 2773.3 jit_solution(1624016202889064237)
XLA Ops:
  2.1 3.0 collective-permute-start
  6.8 18.3 all_gather.3
  25.1 2650.2 %while.20 = (s32[]{:T(128)}, f32[128,32,512]{2,1,0:T(8,128)}, f32[8]{0:T(128)}, bf16[8,64,512]{2,1,0:T(8,128)(2,1)S(1)}, s32[128,8]{0,1:T(8,128)}, /*index=5*/s3...) while((s32[]{:T(128)}, f32[128,32,512]{2,1,0:T(8,128)}, f32[8]{0:T(128)}, ...), condition=%wide.region_1.2_spmd.clone, body=%wide.region_0.1_spmd.clone.sunk | while | flops 8389893 | bytes 21308716 | solution.py:50
  25.9 318.9 %while.21 = (s32[]{:T(128)}, bf16[64,544]{1,0:T(8,128)(2,1)S(1)}, s32[128,2]{0,1:T(2,128)S(1)}, bf16[128,32,512]{2,1,0:T(8,128)(2,1)}, s32[]{:T(128)}) while((s32[]{:T(128)}, bf16[64,544]{1,0:T(8,128)(2,1)S(1)}, s32[128,2]{0,1:T(2,128)S(1)}, bf16[128,32,512]{2,1,0:T(8,128)(2,1)}, s32[]{:T(128)}) %tuple.88), condition=%wide.while_cond, body=%wide.while_body.sunk | while | flops 2 | bytes 66669 | solution.py:43
  31.5 1.9 bitcast_dynamic-update-slice_fusion.2
  34.0 1.9 bitcast_dynamic-update-slice_fusion.2
  36.5 1.9 bitcast_dynamic-update-slice_fusion.2
  39.0 1.9 bitcast_dynamic-update-slice_fusion.2
  41.5 1.9 bitcast_dynamic-update-slice_fusion.2
  44.0 1.9 bitcast_dynamic-update-slice_fusion.2
  46.5 1.9 bitcast_dynamic-update-slice_fusion.2
  49.0 1.9 bitcast_dynamic-update-slice_fusion.2
  51.5 1.9 bitcast_dynamic-update-slice_fusion.2
  54.0 1.9 bitcast_dynamic-update-slice_fusion.2
  56.4 1.9 bitcast_dynamic-update-slice_fusion.2
  58.9 1.9 bitcast_dynamic-update-slice_fusion.2
  61.4 1.9 bitcast_dynamic-update-slice_fusion.2
  63.9 1.9 bitcast_dynamic-update-slice_fusion.2
  66.4 1.9 bitcast_dynamic-update-slice_fusion.2
  78.9 1.9 bitcast_dynamic-update-slice_fusion.2
  81.4 1.9 bitcast_dynamic-update-slice_fusion.2
  83.8 1.9 bitcast_dynamic-update-slice_fusion.2
  86.3 1.9 bitcast_dynamic-update-slice_fusion.2
  88.8 1.9 bitcast_dynamic-update-slice_fusion.2
  91.3 1.9 bitcast_dynamic-update-slice_fusion.2
  93.8 1.9 bitcast_dynamic-update-slice_fusion.2
  96.3 1.9 bitcast_dynamic-update-slice_fusion.2
  98.8 1.9 bitcast_dynamic-update-slice_fusion.2
  346.1 8.2 select_add_fusion.2
  355.1 318.9 %while.21 = (s32[]{:T(128)}, bf16[64,544]{1,0:T(8,128)(2,1)S(1)}, s32[128,2]{0,1:T(2,128)S(1)}, bf16[128,32,512]{2,1,0:T(8,128)(2,1)}, s32[]{:T(128)}) while((s32[]{:T(128)}, bf16[64,544]{1,0:T(8,128)(2,1)S(1)}, s32[128,2]{0,1:T(2,128)S(1)}, bf16[128,32,512]{2,1,0:T(8,128)(2,1)}, s32[]{:T(128)}) %tuple.88), condition=%wide.while_cond, body=%wide.while_body.sunk | while | flops 2 | bytes 66669 | solution.py:43
  675.3 10.6 select_add_fusion.2
  686.7 318.9 %while.21 = (s32[]{:T(128)}, bf16[64,544]{1,0:T(8,128)(2,1)S(1)}, s32[128,2]{0,1:T(2,128)S(1)}, bf16[128,32,512]{2,1,0:T(8,128)(2,1)}, s32[]{:T(128)}) while((s32[]{:T(128)}, bf16[64,544]{1,0:T(8,128)(2,1)S(1)}, s32[128,2]{0,1:T(2,128)S(1)}, bf16[128,32,512]{2,1,0:T(8,128)(2,1)}, s32[]{:T(128)}) %tuple.88), condition=%wide.while_cond, body=%wide.while_body.sunk | while | flops 2 | bytes 66669 | solution.py:43
  1006.9 10.6 select_add_fusion.2
  1018.3 318.9 %while.21 = (s32[]{:T(128)}, bf16[64,544]{1,0:T(8,128)(2,1)S(1)}, s32[128,2]{0,1:T(2,128)S(1)}, bf16[128,32,512]{2,1,0:T(8,128)(2,1)}, s32[]{:T(128)}) while((s32[]{:T(128)}, bf16[64,544]{1,0:T(8,128)(2,1)S(1)}, s32[128,2]{0,1:T(2,128)S(1)}, bf16[128,32,512]{2,1,0:T(8,128)(2,1)}, s32[]{:T(128)}) %tuple.88), condition=%wide.while_cond, body=%wide.while_body.sunk | while | flops 2 | bytes 66669 | solution.py:43
  1338.4 10.6 select_add_fusion.2
  1349.8 318.9 %while.21 = (s32[]{:T(128)}, bf16[64,544]{1,0:T(8,128)(2,1)S(1)}, s32[128,2]{0,1:T(2,128)S(1)}, bf16[128,32,512]{2,1,0:T(8,128)(2,1)}, s32[]{:T(128)}) while((s32[]{:T(128)}, bf16[64,544]{1,0:T(8,128)(2,1)S(1)}, s32[128,2]{0,1:T(2,128)S(1)}, bf16[128,32,512]{2,1,0:T(8,128)(2,1)}, s32[]{:T(128)}) %tuple.88), condition=%wide.while_cond, body=%wide.while_body.sunk | while | flops 2 | bytes 66669 | solution.py:43
  1670.0 10.6 select_add_fusion.2
  1681.4 318.9 %while.21 = (s32[]{:T(128)}, bf16[64,544]{1,0:T(8,128)(2,1)S(1)}, s32[128,2]{0,1:T(2,128)S(1)}, bf16[128,32,512]{2,1,0:T(8,128)(2,1)}, s32[]{:T(128)}) while((s32[]{:T(128)}, bf16[64,544]{1,0:T(8,128)(2,1)S(1)}, s32[128,2]{0,1:T(2,128)S(1)}, bf16[128,32,512]{2,1,0:T(8,128)(2,1)}, s32[]{:T(128)}) %tuple.88), condition=%wide.while_cond, body=%wide.while_body.sunk | while | flops 2 | bytes 66669 | solution.py:43
  2001.6 10.6 select_add_fusion.2
  2013.0 318.9 %while.21 = (s32[]{:T(128)}, bf16[64,544]{1,0:T(8,128)(2,1)S(1)}, s32[128,2]{0,1:T(2,128)S(1)}, bf16[128,32,512]{2,1,0:T(8,128)(2,1)}, s32[]{:T(128)}) while((s32[]{:T(128)}, bf16[64,544]{1,0:T(8,128)(2,1)S(1)}, s32[128,2]{0,1:T(2,128)S(1)}, bf16[128,32,512]{2,1,0:T(8,128)(2,1)}, s32[]{:T(128)}) %tuple.88), condition=%wide.while_cond, body=%wide.while_body.sunk | while | flops 2 | bytes 66669 | solution.py:43
  2333.1 10.6 select_add_fusion.2
  2344.6 318.9 %while.21 = (s32[]{:T(128)}, bf16[64,544]{1,0:T(8,128)(2,1)S(1)}, s32[128,2]{0,1:T(2,128)S(1)}, bf16[128,32,512]{2,1,0:T(8,128)(2,1)}, s32[]{:T(128)}) while((s32[]{:T(128)}, bf16[64,544]{1,0:T(8,128)(2,1)S(1)}, s32[128,2]{0,1:T(2,128)S(1)}, bf16[128,32,512]{2,1,0:T(8,128)(2,1)}, s32[]{:T(128)}) %tuple.88), condition=%wide.while_cond, body=%wide.while_body.sunk | while | flops 2 | bytes 66669 | solution.py:43
  2664.7 10.6 select_add_fusion.2
  2675.3 7.9 copy.10
  2684.6 3.3 collective-permute-start.2
  2689.5 22.8 multiply_add_fusion
  2712.3 56.5 %fusion.24 = bf16[128,32,512]{2,0,1:T(8,128)(2,1)S(1)} fusion(f32[128,32,512]{2,0,1:T(8,128)} %multiply_add_fusion, f32[]{:T(128)} %bitcast.25, f32[]{:T(128)} %bitcast.24, f32[]{:T(128)} %bitcast.23, f32[]{:T(128)} %bitcast.22, f32[]{:T(128)} %bitcast.21, f32[]{:T(128)} %bitcast.20, f32[]{:T(128)} %bitcast.19, f32[]{:T(128)} %bitcast.18, f32[]{:T(128)} %bitcast.17, ...), kind=kLoop, calls=%fused_computation.57 | loop fusion | flops 54525952 | bytes 12582964 | tf_op jit(solution)/shard_map/convert_element_type | solution.py:60
  2768.9 4.4 copy.8
  (3112 shorter events, 2527.7 us)
Async XLA Ops:
  0.8 4.3 collective-permute-start.1
  2.1 3.9 collective-permute-start
  2675.3 12.5 copy-start
  2675.3 13.2 copy-start.1
  2683.3 6.0 collective-permute-start.3
  2684.6 4.9 collective-permute-start.2
where the time goes:
time: 2820 us; the launch traced here: 2770 us
  local copies, waits for them, and re-layouts  2570 us (91%)
  other arithmetic  168 us (6%)
    gather x3072, local copies, waits for them, and re-layouts  2550 us
    add x8, other arithmetic, one_frame(): return acc + weight * moved.astype(jnp.float32)  82.2 us
    convert_element_type x1, other arithmetic, shards(): return result.astype(jnp.bfloat16)  56.5 us
  transfers between devices with their start and end apart: 4, of which 2 were waited for; matrix products, arithmetic and copies ran while one was open for 0% of the time, Pallas kernels for 0%

commit v1 on v0

v1 whole, which is shorter than its diff:
```python
import functools

import jax
import jax.numpy as jnp
import numpy as np
from jax import lax
from jax.experimental import pallas as pl
from jax.experimental.pallas import tpu as pltpu
from jax.sharding import PartitionSpec as P

HALO = 16
RADIUS = 6
TAPS = 2 * RADIUS + 1
FRAMES = 8
RATES = 2 * HALO + 1
GROUP = 4
LANES = 128
FAR = 4096


def frame_moves(frame):
    return [rate * (2 * frame - (FRAMES - 1)) // (FRAMES - 1) for rate in range(-HALO, HALO + 1)]


LOWEST = [min(frame_moves(f)) for f in range(FRAMES)]
HIGHEST = [max(frame_moves(f)) for f in range(FRAMES)]
REACH = [(max(-LOWEST[f], HIGHEST[f]) + RADIUS + 1) // 2 * 2 for f in range(FRAMES)]
OFFSET = [sum(REACH[:f]) for f in range(FRAMES)]
SIDE = sum(REACH)
FIRST = [min(OFFSET[f] // 16, SIDE // 16 - 2) for f in range(FRAMES)]
ENTRIES = [(f, move) for f in range(FRAMES) for move in range(LOWEST[f], HIGHEST[f] + 1)]
BASE = [sum(HIGHEST[i] - LOWEST[i] + 1 for i in range(f)) for f in range(FRAMES)]


def rows_of_sum(rows):
    frame = [f for f in range(FRAMES) for _ in range(rows)]
    row = [y for _ in range(FRAMES) for y in range(rows)]
    for start in (None, rows):
        for f in range(FRAMES):
            frame += [f] * REACH[f]
            row += [(start if start is not None else -REACH[f]) + i for i in range(REACH[f])]
    return np.array(frame), np.array(row)


def prepare_kernel(velocities, slots, rows, height, place, row_moves, col_moves, taps_rows, taps_cols, lane_row, lane_moves,
                   weights_ref, band_ref, edge_ref, list_ref):
    start = place[0] * rows
    inside = lane_row[0:1, :]
    frame_row_ok = jnp.logical_and(inside + start >= 0, inside + start < height)
    y = lax.broadcasted_iota(jnp.int32, (rows, inside.shape[1]), 0)

    def one_rate(rate, _):
        stack_row = inside - lane_moves[pl.ds(rate, 1), :]
        ok = jnp.logical_and(frame_row_ok, jnp.logical_and(stack_row + start >= 0, stack_row + start < height))
        tap = jnp.where(ok, stack_row, FAR) - y
        value = jnp.zeros(tap.shape, jnp.float32)
        for k in range(TAPS):
            value = jnp.where(tap == k - RADIUS, taps_rows[k], value)
        weights_ref[rate] = value.astype(jnp.bfloat16)
        return 0

    lax.fori_loop(0, RATES, one_rate, 0)

    width, wide = band_ref.shape[0] // 2, band_ref.shape[1]
    for at in range(0, width, LANES):
        x = lax.broadcasted_iota(jnp.int32, (LANES, wide), 0) + at
        tap = x - (lax.broadcasted_iota(jnp.int32, (LANES, wide), 1) - HALO)
        value = jnp.zeros(tap.shape, jnp.float32)
        for k in range(TAPS):
            value = jnp.where(tap == k - RADIUS, taps_cols[k], value)
        high = value.astype(jnp.bfloat16)
        band_ref[at:at + LANES, :] = high
        band_ref[width + at:width + at + LANES, :] = (value - high.astype(jnp.float32)).astype(jnp.bfloat16)

    lane = lax.broadcasted_iota(jnp.int32, (LANES, LANES), 1)
    source = lax.broadcasted_iota(jnp.int32, (LANES, LANES), 0)
    move = lane // RADIUS + 1
    at = lane % RADIUS
    left = jnp.where(jnp.logical_and(source < move, move <= HALO), source - at - move, FAR)
    column = source - LANES
    right = jnp.where(jnp.logical_and(column >= -move, move <= HALO), column - (at - RADIUS) + move, FAR)
    for side, tap in enumerate((left, right)):
        value = jnp.zeros(tap.shape, jnp.float32)
        for k in range(TAPS):
            value = jnp.where(tap == k - RADIUS, taps_cols[k], value)
        high = value.astype(jnp.bfloat16)
        edge_ref[side, 0:LANES, :] = high
        edge_ref[side, LANES:, :] = (value - high.astype(jnp.float32)).astype(jnp.bfloat16)

    last = FRAMES - 1
    r_col = row_moves[:, last:last + 1] + HALO
    c_col = col_moves[:, last:last + 1] + HALO
    shape = (velocities, velocities)
    down = lax.broadcasted_iota(jnp.int32, shape, 0)
    across = lax.broadcasted_iota(jnp.int32, shape, 1)
    c_row = jnp.sum(jnp.where(down == across, c_col, 0), axis=0, keepdims=True)
    rank_row = jnp.sum(jnp.where(jnp.logical_and(c_col == c_row, down < across), 1, 0), axis=0, keepdims=True)
    rates = -(-RATES // 8) * 8
    rate_down = lax.broadcasted_iota(jnp.int32, (rates, velocities), 0)
    count_col = jnp.sum(jnp.where(rate_down == c_row, 1, 0), axis=1, keepdims=True)
    groups_col = (count_col + (GROUP - 1)) // GROUP
    before_row = jnp.sum(jnp.where(rate_down < c_row, groups_col, 0), axis=0, keepdims=True)
    slot_row = before_row * GROUP + rank_row
    slot_col = jnp.sum(jnp.where(down == across, slot_row, 0), axis=1, keepdims=True)
    slot_across = lax.broadcasted_iota(jnp.int32, (velocities, slots), 1)
    here = slot_col == slot_across
    which = lax.broadcasted_iota(jnp.int32, (velocities, slots), 0)
    list_ref[...] = jnp.zeros(list_ref.shape, jnp.int32)
    list_ref[0:1, :] = jnp.sum(jnp.where(here, which + 1, 0), axis=0, keepdims=True)
    list_ref[1:2, :] = jnp.sum(jnp.where(here, r_col, 0), axis=0, keepdims=True)
    list_ref[2:3, :] = jnp.sum(jnp.where(here, c_col, 0), axis=0, keepdims=True)
    total = jnp.sum(groups_col, axis=0, keepdims=True)
    list_ref[3:4, :] = jnp.broadcast_to(total, (1, slots))


def main_kernel(rows, width, pieces_count, place, lists, entries, entry_at, frame_weight, *refs):
    pieces = refs[:pieces_count]
    top, bottom, weights, band, edge, out, frames, filtered, outside, table, stage, sem = refs[pieces_count:]
    own = FRAMES // pieces_count
    middle = FRAMES * rows
    block = rows + 64

    for s, piece in enumerate(pieces):
        group = lax.rem(place[1] + pieces_count - s, pieces_count)
        for i in range(own):
            frames[pl.ds(pl.multiple_of((group * own + i) * rows, rows), rows), :] = piece[i]
    frames[middle:middle + SIDE, :] = top[...]
    frames[middle + SIDE:, :] = bottom[...]

    source = frames[...]
    spread = jnp.dot(source, band[:width, :], preferred_element_type=jnp.float32)
    spread += jnp.dot(source, band[width:, :], preferred_element_type=jnp.float32)
    ends = []
    for side, at in enumerate((0, width - LANES)):
        part = source[:, at:at + LANES]
        ends.append(jnp.dot(part, edge[side, :LANES, :], preferred_element_type=jnp.float32)
                    + jnp.dot(part, edge[side, LANES:, :], preferred_element_type=jnp.float32))
    ends = jnp.concatenate(ends, axis=1)
    for f in range(FRAMES):
        w = frame_weight[f]
        filtered[f, 0:rows, :] = (spread[f * rows:(f + 1) * rows] * w).astype(jnp.bfloat16)
        outside[f, 0:rows, :] = (ends[f * rows:(f + 1) * rows] * w).astype(jnp.bfloat16)
        for side in range(2):
            at = middle + side * SIDE + FIRST[f] * 16
            to = rows + 32 * side
            row = lax.broadcasted_iota(jnp.int32, (32, 1), 0) + FIRST[f] * 16
            scale = jnp.where(jnp.logical_and(row >= OFFSET[f], row < OFFSET[f] + REACH[f]), w, 0.0)
            filtered[f, to:to + 32, :] = (spread[at:at + 32] * scale).astype(jnp.bfloat16)
            outside[f, to:to + 32, :] = (ends[at:at + 32] * scale).astype(jnp.bfloat16)

    def one_entry(i, _):
        f = entries[0, i]
        moved = pltpu.roll(filtered[f], entries[1, i], 1)[:, :width]
        fix = outside[f]
        lane = lax.broadcasted_iota(jnp.int32, (block, LANES), 1)
        left = jnp.where(lane < RADIUS, pltpu.roll(fix[:, :LANES], entries[2, i], 1), 0)
        right = jnp.where(lane >= LANES - RADIUS, pltpu.roll(fix[:, LANES:], entries[3, i], 1), 0)
        table[i, :, :LANES] = moved[:, :LANES] - left
        table[i, :, LANES:width - LANES] = moved[:, LANES:width - LANES]
        table[i, :, width - LANES:] = moved[:, width - LANES:] - right
        return 0

    lax.fori_loop(0, len(ENTRIES), one_entry, 0)

    def one_group(k, _):
        c = lists[2, k * GROUP]
        at = [entry_at[f, c] for f in range(FRAMES)]
        parts = [table[at[f], 0:rows, :] for f in range(FRAMES)]
        for side in range(2):
            for tile in range(SIDE // 16):
                total = None
                for f in range(FRAMES):
                    for half in range(2):
                        low = (FIRST[f] + half) * 16
                        if FIRST[f] + half == tile and low < OFFSET[f] + REACH[f] and low + 16 > OFFSET[f]:
                            at_row = rows + 32 * side + 16 * half
                            piece = table[at[f], at_row:at_row + 16, :]
                            total = piece if total is None else total + piece
                parts.append(total)
        shifted = jnp.concatenate(parts, axis=0)
        chosen = jnp.concatenate([weights[lists[1, k * GROUP + i]] for i in range(GROUP)], axis=0)
        result = jnp.dot(chosen, shifted, preferred_element_type=jnp.float32).astype(jnp.bfloat16)
        for i in range(GROUP):
            v = lists[0, k * GROUP + i] - 1

            @pl.when(v >= 0)
            def _():
                stage[v] = result[i * rows:(i + 1) * rows]
                pltpu.make_async_copy(stage.at[v], out.at[v], sem).start()

        return 0

    lax.fori_loop(0, lists[3, 0], one_group, 0)
    pltpu.make_async_copy(stage, out, sem).wait()


def shards(frames, row_shifts, column_shifts, frame_inverse_weight, psf_rows, psf_cols):
    own, rows, width = frames.shape
    velocities = row_shifts.shape[0]
    groups = lax.axis_size("frame")
    bands = lax.axis_size("tile")
    height = bands * rows
    depth = FRAMES * rows + 2 * SIDE
    most = min(RATES, velocities)
    slots = -(-(velocities + (GROUP - 1) * most) // LANES) * LANES
    wide = width + LANES
    place = jnp.stack([lax.axis_index("tile"), lax.axis_index("frame")]).astype(jnp.int32)

    lane_frame, lane_row = rows_of_sum(rows)
    lane_moves = np.array([[frame_moves(f)[rate] for f in lane_frame] for rate in range(RATES)], np.int32)
    lane_moves = np.pad(lane_moves, ((0, -RATES % 8), (0, 0)))
    lane_rows = np.broadcast_to(lane_row.astype(np.int32), (8, depth))

    smem = pl.BlockSpec(memory_space=pltpu.SMEM)
    vmem = pl.BlockSpec(memory_space=pltpu.VMEM)
    weights, band, edge, lists = pl.pallas_call(
        functools.partial(prepare_kernel, velocities, slots, rows, height),
        out_shape=(
            jax.ShapeDtypeStruct((RATES, rows, depth), jnp.bfloat16),
            jax.ShapeDtypeStruct((2 * width, wide), jnp.bfloat16),
            jax.ShapeDtypeStruct((2, 2 * LANES, LANES), jnp.bfloat16),
            jax.ShapeDtypeStruct((8, slots), jnp.int32),
        ),
        in_specs=[smem, vmem, vmem, smem, smem, vmem, vmem],
        out_specs=(vmem, vmem, vmem, vmem),
        name="prepare",
    )(place, row_shifts, column_shifts, psf_rows, psf_cols, jnp.asarray(lane_rows), jnp.asarray(lane_moves))

    pieces = [frames]
    for s in range(1, groups):
        pieces.append(lax.ppermute(frames, "frame", [(i, (i + s) % groups) for i in range(groups)]))

    ordered = jnp.concatenate(pieces[::-1], axis=0)
    ordered = jnp.roll(ordered, (place[1] + 1) * own, axis=0)
    low = jnp.concatenate([ordered[f, rows - REACH[f]:] for f in range(FRAMES)], axis=0)
    high = jnp.concatenate([ordered[f, :REACH[f]] for f in range(FRAMES)], axis=0)
    top = lax.ppermute(low, "tile", [(i, (i + 1) % bands) for i in range(bands)])
    bottom = lax.ppermute(high, "tile", [((i + 1) % bands, i) for i in range(bands)])

    entries = np.zeros((8, -(-len(ENTRIES) // LANES) * LANES), np.int32)
    for i, (f, move) in enumerate(ENTRIES):
        entries[0, i] = f
        entries[1, i] = wide - (HALO + move)
        entries[2, i] = (LANES - RADIUS * (move - 1 if move > 0 else HALO)) % LANES
        entries[3, i] = (LANES - RADIUS - RADIUS * (-move - 1 if move < 0 else HALO)) % LANES
    entry_at = np.array([[BASE[f] + move - LOWEST[f] for move in frame_moves(f)] for f in range(FRAMES)], np.int32)
    entry_at = np.pad(entry_at, ((0, 0), (0, LANES - RATES)))

    block = rows + 64
    return pl.pallas_call(
        functools.partial(main_kernel, rows, width, groups),
        out_shape=jax.ShapeDtypeStruct((velocities, rows, width), jnp.bfloat16),
        in_specs=[smem] * 5 + [vmem] * (groups + 5),
        out_specs=pl.BlockSpec(memory_space=pl.ANY),
        scratch_shapes=[
            pltpu.VMEM((depth, width), jnp.bfloat16),
            pltpu.VMEM((FRAMES, block, wide), jnp.bfloat16),
            pltpu.VMEM((FRAMES, block, 2 * LANES), jnp.bfloat16),
            pltpu.VMEM((len(ENTRIES), block, width), jnp.bfloat16),
            pltpu.VMEM((velocities, rows, width), jnp.bfloat16),
            pltpu.SemaphoreType.DMA,
        ],
        compiler_params=pltpu.CompilerParams(vmem_limit_bytes=56 * 2**20),
        name="track",
    )(place, lists, jnp.asarray(entries), jnp.asarray(entry_at), frame_inverse_weight, *pieces, top, bottom, weights, band, edge)


def solution(mesh):
    return jax.shard_map(
        shards,
        mesh=mesh,
        in_specs=(P("frame", "tile", None), P("frame", None), P("frame", None), P(), P(), P()),
        out_specs=P("frame", "tile", None),
        check_vma=False,
    )
```

time: 2820 us -> 61.5 us (0.02); the launches traced: 2770 us -> 61.4 us
  local copies, waits for them, and re-layouts: 2570 us -> 5.8 us
  other arithmetic: 168 us -> 0.61 us
  Pallas kernels: 0 us -> 40.4 us
    gather x3072 -> x0, local copies, waits for them, and re-layouts: 2550 us -> none
    add x9 -> x0, other arithmetic: 105 us -> none  [the longest x8 82.2 us: one_frame(): return acc + weight * moved.astype(jnp.float32)]
    convert_element_type x1 -> x0, other arithmetic: 56.5 us -> none  [shards(): return result.astype(jnp.bfloat16)]
    pallas_call x0 -> x2, Pallas kernels: none -> 40.4 us  [the longest x1 35.3 us: shards(): pl.pallas_call(functools.partial(main_kernel, rows, width, groups), out_s...]
  transfers between devices with their start and end apart: 4 -> 5, of which waited for: 2 -> 2; matrix products, arithmetic and copies ran while one was open for 0% -> 5% of each run, Pallas kernels for 0% -> 8%
where the time goes in v1:
time: 61.5 us; the launch traced here: 61.4 us
  Pallas kernels  40.4 us (66%)
  starting transfers between devices  8.79 us (14%)
  local copies, waits for them, and re-layouts  5.8 us (9%)
  waiting for transfers between devices  5.66 us (9%)
    pallas_call x1, Pallas kernels, shards(): pl.pallas_call(functools.partial(main_kernel, rows, width, groups), out_s...  35.3 us
    ppermute x3, starting transfers between devices, shards(): lax.ppermute(frames, 'frame', [(i, (i + s) % groups) for i in range(group...  6.12 us
    ppermute x3, waiting for transfers between devices, shards(): lax.ppermute(frames, 'frame', [(i, (i + s) % groups) for i in range(group...  5.66 us
    pallas_call x1, Pallas kernels, shards(): pl.pallas_call(functools.partial(prepare_kernel, velocities, slots, rows,...  5.07 us
    unnamed x25, local copies, waits for them, and re-layouts  3.05 us
    ppermute x1, starting transfers between devices, shards(): lax.ppermute(high, 'tile', [((i + 1) % bands, i) for i in range(bands)])  2.61 us
  transfers between devices with their start and end apart: 5, of which 2 were waited for; matrix products, arithmetic and copies ran while one was open for 5% of the time, Pallas kernels for 8%

profile of v1, /device:TPU:0, one launch (start us, length us, event | category | flops | bytes accessed | tf_op | source)
XLA Modules:
  0.0 61.4 jit_solution(9220034940601414747)
XLA Ops:
  0.0 0.0 copy-start.7
  0.0 0.0 copy-start.5
  0.0 0.0 copy-start.6
  0.0 5.1 %collective-permute-start.2 = (bf16[2,32,512]{2,1,0:T(8,128)(2,1)}, bf16[2,32,512]{2,1,0:T(8,128)(2,1)S(1)}, u32[]{:S(2)}, u32[]{:S(2)}) collective-permute-start(bf16[2,32,512]{2,1,0:T(8,128)(2,1)} %refs_0_.1), channel_id=1, source_target_pairs={{0,3},{1,0},{2,1},{3,2},{4,7},{5,4},{6,5},{7,6},{8,11},{9,8},{10,9... | collective-permute-start | bytes 196616 | tf_op jit(solution)/shard_map/ppermute | solution.py:231
  5.1 0.0 collective-permute-start.1
  5.1 1.0 %collective-permute-start = (bf16[2,32,512]{2,1,0:T(8,128)(2,1)}, bf16[2,32,512]{2,1,0:T(8,128)(2,1)S(1)}, u32[]{:S(2)}, u32[]{:S(2)}) collective-permute-start(bf16[2,32,512]{2,1,0:T(8,128)(2,1)} %refs_0_.1), channel_id=1, source_target_pairs={{0,1},{1,2},{2,3},{3,0},{4,5},{5,6},{6,7},{7,4},{8,9},{9,10},{10,1... | collective-permute-start | bytes 196616 | tf_op jit(solution)/shard_map/ppermute | solution.py:231
  6.1 1.8 %collective-permute-done.2.refs_3_ = bf16[2,32,512]{2,1,0:T(8,128)(2,1)S(1)} collective-permute-done((bf16[2,32,512]{2,1,0:T(8,128)(2,1)}, bf16[2,32,512]{2,1,0:T(8,128)(2,1)S(1)}, u32[]{:S(2)}, u32[]{:S(2)}) %collective-permute-start.2) | collective-permute-done | bytes 65568 | tf_op jit(solution)/shard_map/ppermute | solution.py:231
  7.9 0.0 copy-start
  7.9 3.9 %collective-permute-done.1.refs_2_ = bf16[2,32,512]{2,1,0:T(8,128)(2,1)S(1)} collective-permute-done((bf16[2,32,512]{2,1,0:T(8,128)(2,1)}, bf16[2,32,512]{2,1,0:T(8,128)(2,1)S(1)}, u32[]{:S(2)}, u32[]{:S(2)}) %collective-permute-start.1) | collective-permute-done | bytes 65568 | tf_op jit(solution)/shard_map/ppermute | solution.py:231
  11.8 0.0 copy-start.1
  11.8 0.0 collective-permute-done.refs_1_
  11.8 0.0 copy-start.2
  11.8 0.9 %constant_dynamic-update-slice_fusion.4 = bf16[16,32,512]{2,1,0:T(8,128)(2,1)S(1)} fusion(bf16[16,32,512]{2,1,0:T(8,128)(2,1)S(1)} %constant_dynamic-update-slice_fusion.5, bf16[2,32,512]{2,1,0:T(8,128)(2,1)} %refs_0_.1), kind=kLoop, calls=%fused_computation.12 | loop fusion | bytes 131072
  12.7 0.8 %constant_dynamic-update-slice_fusion = bf16[16,32,512]{2,1,0:T(8,128)(2,1)S(1)} fusion(bf16[16,32,512]{2,1,0:T(8,128)(2,1)S(1)} %constant_dynamic-update-slice_fusion.1, bf16[2,32,512]{2,1,0:T(8,128)(2,1)} %refs_0_.1), kind=kLoop, calls=%fused_computation.8 | loop fusion | bytes 131072 | tf_op jit(solution)/shard_map/jit(_roll_dynamic)/concatenate | solution.py:234
  13.7 0.6 concatenate.13
  14.3 0.1 collective-permute-start.3
  14.4 0.6 concatenate.14
  15.0 2.6 %collective-permute-start.4 = (bf16[128,512]{1,0:T(8,128)(2,1)S(1)}, bf16[128,512]{1,0:T(8,128)(2,1)S(1)}, u32[]{:S(2)}, u32[]{:S(2)}) collective-permute-start(bf16[128,512]{1,0:T(8,128)(2,1)S(1)} %concatenate.14), channel_id=1, source_target_pairs={{4,0},{8,4},{12,8},{16,12},{20,16},{24,20},{28,24},{0,28},{5,1},{9... | collective-permute-start | bytes 393224 | tf_op jit(solution)/shard_map/ppermute | solution.py:238
  17.6 0.0 copy-done.5
  17.6 0.7 %copy.11.row_moves = s32[128,8]{1,0:T(8,128)} copy(s32[128,8]{0,1:T(8,128)S(1)} %copy-done.5) | data formatting | bytes 8192 | tf_op args[1]
  18.3 0.0 copy-done.6
  18.3 0.7 %copy.12.col_moves = s32[128,8]{1,0:T(8,128)} copy(s32[128,8]{0,1:T(8,128)S(1)} %copy-done.6) | data formatting | bytes 8192 | tf_op args[2]
  19.1 0.6 pad_add_fusion.place
  19.7 0.0 copy-done.7
  19.7 0.6 jit_solution_.3.lane_row
  20.3 5.1 %prepare.1 = (bf16[33,32,512]{2,1,0:T(8,128)(2,1)}, bf16[1024,640]{1,0:T(8,128)(2,1)}, bf16[2,256,128]{2,1,0:T(8,128)(2,1)}, s32[8,256]{1,0:T(8,128)}) custom-call(s32[2]{0:T(128)} %pad_add_fusion.place, s32[128,8]{1,0:T(8,128)} %copy.11.row_moves, s32[128,8]{1,0:T(8,128)} %copy.12.col_moves, f32[13]{0:T(128)} %taps_rows.1, f32[13]{0:T(128)} %taps_cols.1, ...), custom_call_target="tpu_custom_call" | custom-call | tf_op jit(solution)/shard_map/prepare/pallas_call | solution.py:216
  25.4 0.0 copy-done
  25.4 0.0 collective-permute-done.3.refs_4_
  25.4 0.0 copy-start.3
  25.4 0.0 collective-permute-done.4.refs_5_
  25.4 0.0 copy-start.4
  25.4 0.0 copy-done.1
  25.4 0.0 copy-done.2
  25.4 0.6 copy-done.3
  26.0 0.1 copy-done.4
  26.1 35.3 %track.1 = bf16[128,32,512]{2,1,0:T(8,128)(2,1)} custom-call(s32[2]{0:T(128)} %pad_add_fusion.place, s32[8,256]{1,0:T(8,128)} %get-tuple-element.9.lists, s32[8,256]{1,0:T(8,128)} %constant.45.clone.entries, s32[8,128]{1,0:T(8,128)} %constant.46.clone.entry_at, f32[8]{0:T(128)} %frame_weight.1, bf16[2,32,512]{2,1,0:T(8,128)(2,1)} %refs_0_.1, ...), custom_call_target="tpu_custom_call" | custom-call | tf_op jit(solution)/shard_map/track/pallas_call | solution.py:250
  (10 shorter events, 0.2 us)
Async XLA Ops:
  0.0 19.7 %copy-start.7 = (s32[512]{0:T(512)S(1)}, s32[512]{0:T(512)}, u32[]{:S(2)}) copy-start(s32[512]{0:T(512)} %constant.43.clone) | copy-start | bytes 6148
  0.0 17.6 %copy-start.5 = (s32[128,8]{0,1:T(8,128)S(1)}, s32[128,8]{0,1:T(8,128)}, u32[]{:S(2)}) copy-start(s32[128,8]{0,1:T(8,128)} %param.11) | copy-start | bytes 12292
  0.0 18.3 %copy-start.6 = (s32[128,8]{0,1:T(8,128)S(1)}, s32[128,8]{0,1:T(8,128)}, u32[]{:S(2)}) copy-start(s32[128,8]{0,1:T(8,128)} %param.12) | copy-start | bytes 12292
  0.0 7.9 %collective-permute-start.2 = (bf16[2,32,512]{2,1,0:T(8,128)(2,1)}, bf16[2,32,512]{2,1,0:T(8,128)(2,1)S(1)}, u32[]{:S(2)}, u32[]{:S(2)}) collective-permute-start(bf16[2,32,512]{2,1,0:T(8,128)(2,1)} %refs_0_.1), channel_id=1, source_target_pairs={{0,3},{1,0},{2,1},{3,2},{4,7},{5,4},{6,5},{7,6},{8,11},{9,8},{10,9... | collective-permute-start | bytes 196616 | tf_op jit(solution)/shard_map/ppermute | solution.py:231
  5.1 6.7 %collective-permute-start.1 = (bf16[2,32,512]{2,1,0:T(8,128)(2,1)}, bf16[2,32,512]{2,1,0:T(8,128)(2,1)S(1)}, u32[]{:S(2)}, u32[]{:S(2)}) collective-permute-start(bf16[2,32,512]{2,1,0:T(8,128)(2,1)} %refs_0_.1), channel_id=1, source_target_pairs={{0,2},{1,3},{2,0},{3,1},{4,6},{5,7},{6,4},{7,5},{8,10},{9,11},{10,... | collective-permute-start | bytes 196616 | tf_op jit(solution)/shard_map/ppermute | solution.py:231
  5.1 6.7 %collective-permute-start = (bf16[2,32,512]{2,1,0:T(8,128)(2,1)}, bf16[2,32,512]{2,1,0:T(8,128)(2,1)S(1)}, u32[]{:S(2)}, u32[]{:S(2)}) collective-permute-start(bf16[2,32,512]{2,1,0:T(8,128)(2,1)} %refs_0_.1), channel_id=1, source_target_pairs={{0,1},{1,2},{2,3},{3,0},{4,5},{5,6},{6,7},{7,4},{8,9},{9,10},{10,1... | collective-permute-start | bytes 196616 | tf_op jit(solution)/shard_map/ppermute | solution.py:231
  7.9 17.4 %copy-start = (bf16[2,32,512]{2,1,0:T(8,128)(2,1)}, bf16[2,32,512]{2,1,0:T(8,128)(2,1)S(1)}, u32[]{:S(2)}) copy-start(bf16[2,32,512]{2,1,0:T(8,128)(2,1)S(1)} %collective-permute-done.2.refs_3_) | copy-start | bytes 196612
  11.8 13.6 %copy-start.1 = (bf16[2,32,512]{2,1,0:T(8,128)(2,1)}, bf16[2,32,512]{2,1,0:T(8,128)(2,1)S(1)}, u32[]{:S(2)}) copy-start(bf16[2,32,512]{2,1,0:T(8,128)(2,1)S(1)} %collective-permute-done.1.refs_2_) | copy-start | bytes 196612
  11.8 13.6 %copy-start.2 = (bf16[2,32,512]{2,1,0:T(8,128)(2,1)}, bf16[2,32,512]{2,1,0:T(8,128)(2,1)S(1)}, u32[]{:S(2)}) copy-start(bf16[2,32,512]{2,1,0:T(8,128)(2,1)S(1)} %collective-permute-done.refs_1_) | copy-start | bytes 196612
  14.3 11.0 %collective-permute-start.3 = (bf16[128,512]{1,0:T(8,128)(2,1)S(1)}, bf16[128,512]{1,0:T(8,128)(2,1)S(1)}, u32[]{:S(2)}, u32[]{:S(2)}) collective-permute-start(bf16[128,512]{1,0:T(8,128)(2,1)S(1)} %concatenate.13), channel_id=1, source_target_pairs={{0,4},{4,8},{8,12},{12,16},{16,20},{20,24},{24,28},{28,0},{1,5},{5... | collective-permute-start | bytes 393224 | tf_op jit(solution)/shard_map/ppermute | solution.py:237
  15.0 10.4 %collective-permute-start.4 = (bf16[128,512]{1,0:T(8,128)(2,1)S(1)}, bf16[128,512]{1,0:T(8,128)(2,1)S(1)}, u32[]{:S(2)}, u32[]{:S(2)}) collective-permute-start(bf16[128,512]{1,0:T(8,128)(2,1)S(1)} %concatenate.14), channel_id=1, source_target_pairs={{4,0},{8,4},{12,8},{16,12},{20,16},{24,20},{28,24},{0,28},{5,1},{9... | collective-permute-start | bytes 393224 | tf_op jit(solution)/shard_map/ppermute | solution.py:238
  25.4 0.7 %copy-start.3 = (bf16[128,512]{1,0:T(8,128)(2,1)}, bf16[128,512]{1,0:T(8,128)(2,1)S(1)}, u32[]{:S(2)}) copy-start(bf16[128,512]{1,0:T(8,128)(2,1)S(1)} %collective-permute-done.3.refs_4_) | copy-start | bytes 393220
  25.4 0.7 %copy-start.4 = (bf16[128,512]{1,0:T(8,128)(2,1)}, bf16[128,512]{1,0:T(8,128)(2,1)S(1)}, u32[]{:S(2)}) copy-start(bf16[128,512]{1,0:T(8,128)(2,1)S(1)} %collective-permute-done.4.refs_5_) | copy-start | bytes 393220
